TPU v7x, 256 devices: a whole 4x4x8 slice. The times are simulated.
256 devices in a mesh: tm: 32 (over z_hi, x, core), space: 8 (over z_lo, y).
Axes of the slice: x: 4, y: 4, z: 8 (z_hi: 4, z_lo: 2; z = z_hi * 2 + z_lo), core: 2. Of those that a mesh axis runs over, the one named last changes fastest.
Arguments:
- initial: float32 [4, 65536], P(None, 'space'), may hold values from -6 to 6
- sources: float32 [32, 4, 65536], P('tm', None, 'space'), may hold values from -6 to 6
- operator: bfloat16 [128, 4, 512, 512], P('space'), may hold values from -0.015625 to 0.015625
- col_blocks: int32 [128, 4], P('space'), may hold values from 0 to 127, as said below
- coarse_inv: float32 [128, 512, 512], P('space'), may hold values from -0.5 to 0.8
Outputs:
- ends: float32 [32, 4, 65536], P('tm', None, 'space')
Inputs may be any that keep to these rules, and one draw needn't show every extreme that they name: `col_blocks`: block row r lists block r, blocks r - 1 and r + 1, and one of r - 2 and r + 2, all modulo 128, in a drawn order.
All inputs are finite; a program needn't handle non-finite values.
Results may differ from a plain program's by a relative error of at most 0.00058.
Values may be sent and summed in bfloat16 or wider, within the bound.
A program may use at most 256 MiB of HBM per device.

v0:
```python
import jax
import jax.numpy as jnp
from jax import lax
from jax.sharding import PartitionSpec as P

HB = 2
FINE_STEPS = 8


def padded_2(cells, sides, width):
    for axis, dim in sides:
        count = lax.axis_size(axis)
        head = lax.slice_in_dim(cells, 0, width, axis=dim)
        tail = lax.slice_in_dim(cells, cells.shape[dim] - width, cells.shape[dim], axis=dim)
        cells = jnp.concatenate(
            [
                lax.ppermute(tail, axis, [(i, (i + 1) % count) for i in range(count)]),
                cells,
                lax.ppermute(head, axis, [((i + 1) % count, i) for i in range(count)]),
            ],
            axis=dim,
        )
    return cells


def shifted(value, axis, steps):
    count = lax.axis_size(axis)
    first, last = (max(0, -steps), min(count, count - steps))
    return lax.ppermute(value, axis, [(source, source + steps) for source in range(first, last)])


def coarse_apply(matrix, current):
    tracer_count = current.shape[0]
    block_count, block_size = (matrix.shape[0], matrix.shape[1])
    stacked = current.reshape(tracer_count, block_count, block_size)
    result = jnp.einsum("rab,trb->tra", matrix, stacked, precision=lax.Precision.HIGHEST)
    return result.reshape(tracer_count, block_count * block_size)


def fine_step(current, operator, local_cols, forcing_share):
    tracer_count = current.shape[0]
    block_count, block_size = (operator.shape[0], operator.shape[2])
    rounded = current.astype(jnp.bfloat16).reshape(tracer_count, block_count, block_size)
    padded = padded_2(rounded, (("space", 1),), HB)
    picked = jnp.take(padded, local_cols, axis=1)
    change = jnp.einsum("rjab,trjb->tra", operator, picked, preferred_element_type=jnp.float32)
    return current + change.reshape(current.shape) + forcing_share


def coarse_pass(initial, increment, coarse_inv):
    slice_count = lax.axis_size("tm")
    own_slice = lax.axis_index("tm")

    def refresh(values):
        arrived, unused_anchor, unused_finish = values
        return (arrived, coarse_apply(coarse_inv, arrived) + increment)

    def keep(values):
        unused_arrived, anchor, finish = values
        return (anchor, finish)

    def advance(turn_index, carried):
        anchor, finish = carried
        incoming = shifted(finish, "tm", 1)
        return lax.cond(turn_index + 1 == own_slice, refresh, keep, (incoming, anchor, finish))

    first_finish = coarse_apply(coarse_inv, initial) + increment
    return lax.fori_loop(0, slice_count - 1, advance, (initial, first_finish))


def local(initial, sources, operator, col_blocks, coarse_inv):
    forcing = sources[0]
    forced = coarse_apply(coarse_inv, forcing)
    anchor, unused_end = coarse_pass(initial, forced, coarse_inv)
    block_count = col_blocks.shape[0]
    first_block = lax.axis_index("space") * block_count
    total_blocks = block_count * lax.axis_size("space")
    offset = jnp.mod(col_blocks - first_block, total_blocks)
    offset = jnp.where(offset >= total_blocks - HB, offset - total_blocks, offset)
    local_cols = offset + HB
    forcing_share = forcing / FINE_STEPS
    current = anchor
    for repeat in range(FINE_STEPS):
        current = fine_step(current, operator, local_cols, forcing_share)
    jump = current - coarse_apply(coarse_inv, anchor)
    unused_anchor, finish = coarse_pass(initial, jump, coarse_inv)
    return finish[None]


def solution(mesh):
    placed = (
        P(None, "space"),
        P("tm", None, "space"),
        P("space", None, None, None),
        P("space", None),
        P("space", None, None),
    )
    return jax.shard_map(
        local, mesh=mesh, in_specs=placed, out_specs=P("tm", None, "space"), check_vma=False
    )
```

profile of v0, /device:TPU:231, one launch (start us, length us, event | category | flops | bytes accessed | tf_op | source)
XLA Modules:
  0.0 1309.1 jit_solution(6352288497425610677)
XLA Ops:
  0.9 17.2 %fusion.69 = f32[16,4,512]{2,1,0:T(4,128)S(1)} fusion(f32[4,16,512]{2,0,1:T(4,128)S(1)} %bitcast.164, f32[16,512,512]{2,1,0:T(8,128)} %param.19), kind=kOutput, calls=%fused_computation.100 | convolution fusion | flops 201326592 | bytes 17039360 | tf_op jit(solution)/shard_map/rab,trb->tra/dot_general | solution.py:36
  18.1 17.2 %fusion.70 = f32[16,4,512]{2,1,0:T(4,128)S(1)} fusion(f32[4,16,512]{2,0,1:T(4,128)} %bitcast.161, f32[16,512,512]{2,1,0:T(8,128)} %param.19), kind=kOutput, calls=%fused_computation.101 | convolution fusion | flops 201326592 | bytes 17039360 | tf_op jit(solution)/shard_map/rab,trb->tra/dot_general | solution.py:36
  35.4 670.2 %while.31 = (s32[]{:T(128)}, f32[4,8192]{1,0:T(4,128)S(1)}, f32[4,8192]{1,0:T(4,128)S(1)}, s32[]{:T(128)}, f32[16,512,512]{2,1,0:T(8,128)}, /*index=5*/f32[4,8192]{1,0:T(4,128)S(1)}, s32[]{:T(128)}) while((s32[]{:T(128)}, f32[4,8192]{1,0:T(4,128)S(1)}, f32[4,8192]{1,0:T(4,128)S(1)}, s32[]{:T(128)}, f32[16,512,512]{2,1,0:T(8,128)}, ...), condition=%wide.region_3.0_spmd, body=%wide.region_0.0_spmd.sunk | while | flops 201359360 | bytes 18219204 | solution.py:68
  123.3 9.3 collective-permute-done
  133.9 9.3 collective-permute-done
  155.0 9.3 collective-permute-done
  165.6 9.3 collective-permute-done
  186.8 9.3 collective-permute-done
  294.3 394.0 %collective-permute-done = f32[4,8192]{1,0:T(4,128)S(1)} collective-permute-done((f32[4,8192]{1,0:T(4,128)S(1)}, f32[4,8192]{1,0:T(4,128)S(1)}, u32[]{:S(2)}, u32[]{:S(2)}) %collective-permute-start) | collective-permute-done | bytes 131104 | tf_op jit(solution)/shard_map/while/body/eval_jaxpr/ppermute | solution.py:29
  688.3 17.3 %conditional.4 = ((f32[4,8192]{1,0:T(4,128)S(1)}, f32[4,8192]{1,0:T(4,128)S(1)})) conditional(s32[]{:T(128)} %convert_element_type.55, (f32[4,8192]{1,0:T(4,128)S(1)}, f32[4,8192]{1,0:T(4,128)S(1)}) %tuple.84, (f32[4,8192]{1,0:T(4,128)S(1)}, f32[16,512,512]{2,1,0:T(8,128)}, f32[4,8192]{1,0:T(4,128)S(1)}) %tuple.85), branch_computations={%region_1.0_spmd, %region_2.0_spmd} | conditional | flops 201359360 | bytes 17694744 | solution.py:65
  688.3 17.2 %fusion.67 = f32[16,4,512]{2,1,0:T(4,128)S(1)} fusion(f32[4,16,512]{2,0,1:T(4,128)S(1)} %bitcast.160, f32[16,512,512]{2,1,0:T(8,128)} %get-tuple-element.223), kind=kOutput, calls=%fused_computation.98 | convolution fusion | flops 201326592 | bytes 17039360 | tf_op jit(solution)/shard_map/while/body/eval_jaxpr/cond/branch_1_fun/rab,trb->tra/dot_general | solution.py:36
  711.2 14.0 %fusion.14 = f32[16,4,512,1]{2,1,3,0:T(4,128)S(1)} fusion(bf16[16,4,512,512]{3,2,1,0:T(8,128)(2,1)} %param.17, bf16[16,4,4,512]{3,2,1,0:T(4,128)(2,1)S(1)} %bitcast.176, pred[16,4]{1,0:T(8,128)(4,1)S(1)} %copy.39), kind=kOutput, calls=%fused_computation.22 | convolution fusion | flops 134348800 | bytes 33947712 | tf_op jit(solution)/shard_map/rjab,trjb->tra/dot_general | solution.py:46
  730.9 14.0 %fusion.12 = f32[16,4,512,1]{2,1,3,0:T(4,128)S(1)} fusion(bf16[16,4,512,512]{3,2,1,0:T(8,128)(2,1)} %param.17, bf16[16,4,4,512]{3,2,1,0:T(4,128)(2,1)S(1)} %bitcast.177, pred[16,4]{1,0:T(8,128)(4,1)S(1)} %copy.39), kind=kOutput, calls=%fused_computation.20 | convolution fusion | flops 134348800 | bytes 33947712 | tf_op jit(solution)/shard_map/rjab,trjb->tra/dot_general | solution.py:46
  750.8 14.0 %fusion.10 = f32[16,4,512,1]{2,1,3,0:T(4,128)S(1)} fusion(bf16[16,4,512,512]{3,2,1,0:T(8,128)(2,1)} %param.17, bf16[16,4,4,512]{3,2,1,0:T(4,128)(2,1)S(1)} %bitcast.178, pred[16,4]{1,0:T(8,128)(4,1)S(1)} %copy.39), kind=kOutput, calls=%fused_computation.18 | convolution fusion | flops 134348800 | bytes 33947712 | tf_op jit(solution)/shard_map/rjab,trjb->tra/dot_general | solution.py:46
  770.5 14.0 %fusion.8 = f32[16,4,512,1]{2,1,3,0:T(4,128)S(1)} fusion(bf16[16,4,512,512]{3,2,1,0:T(8,128)(2,1)} %param.17, bf16[16,4,4,512]{3,2,1,0:T(4,128)(2,1)S(1)} %bitcast.179, pred[16,4]{1,0:T(8,128)(4,1)S(1)} %copy.39), kind=kOutput, calls=%fused_computation.16 | convolution fusion | flops 134348800 | bytes 33947712 | tf_op jit(solution)/shard_map/rjab,trjb->tra/dot_general | solution.py:46
  790.3 14.0 %fusion.6 = f32[16,4,512,1]{2,1,3,0:T(4,128)S(1)} fusion(bf16[16,4,512,512]{3,2,1,0:T(8,128)(2,1)} %param.17, bf16[16,4,4,512]{3,2,1,0:T(4,128)(2,1)S(1)} %bitcast.180, pred[16,4]{1,0:T(8,128)(4,1)S(1)} %copy.39), kind=kOutput, calls=%fused_computation.14 | convolution fusion | flops 134348800 | bytes 33947712 | tf_op jit(solution)/shard_map/rjab,trjb->tra/dot_general | solution.py:46
  810.0 14.0 %fusion.4 = f32[16,4,512,1]{2,1,3,0:T(4,128)S(1)} fusion(bf16[16,4,512,512]{3,2,1,0:T(8,128)(2,1)} %param.17, bf16[16,4,4,512]{3,2,1,0:T(4,128)(2,1)S(1)} %bitcast.181, pred[16,4]{1,0:T(8,128)(4,1)S(1)} %copy.39), kind=kOutput, calls=%fused_computation.12 | convolution fusion | flops 134348800 | bytes 33947712 | tf_op jit(solution)/shard_map/rjab,trjb->tra/dot_general | solution.py:46
  830.2 14.0 %fusion.2 = f32[16,4,512,1]{2,1,3,0:T(4,128)S(1)} fusion(bf16[16,4,512,512]{3,2,1,0:T(8,128)(2,1)} %param.17, bf16[16,4,4,512]{3,2,1,0:T(4,128)(2,1)S(1)} %bitcast.182, pred[16,4]{1,0:T(8,128)(4,1)S(1)} %copy.39), kind=kOutput, calls=%fused_computation.10 | convolution fusion | flops 134348800 | bytes 33947712 | tf_op jit(solution)/shard_map/rjab,trjb->tra/dot_general | solution.py:46
  848.1 17.2 %fusion.71 = f32[16,4,512]{2,1,0:T(4,128)S(1)} fusion(f32[4,16,512]{2,0,1:T(4,128)S(1)} %bitcast.165, f32[16,512,512]{2,1,0:T(8,128)} %get-tuple-element.412), kind=kOutput, calls=%fused_computation.102 | convolution fusion | flops 201326592 | bytes 17039360 | tf_op jit(solution)/shard_map/rab,trb->tra/dot_general | solution.py:36
  866.2 14.0 %fusion = f32[16,4,512,1]{2,1,3,0:T(4,128)S(1)} fusion(bf16[16,4,512,512]{3,2,1,0:T(8,128)(2,1)} %param.17, bf16[16,4,4,512]{3,2,1,0:T(4,128)(2,1)S(1)} %bitcast.175, pred[16,4]{1,0:T(8,128)(4,1)S(1)} %copy.39), kind=kOutput, calls=%fused_computation.8 | convolution fusion | flops 134348800 | bytes 33947712 | tf_op jit(solution)/shard_map/rjab,trjb->tra/dot_general | solution.py:46
  880.3 428.0 %while.32 = (s32[]{:T(128)}, f32[4,8192]{1,0:T(4,128)S(1)}, s32[]{:T(128)}, f32[16,512,512]{2,1,0:T(8,128)}, f32[4,8192]{1,0:T(4,128)S(1)}, /*index=5*/s32[]{:T(128)}) while((s32[]{:T(128)}, f32[4,8192]{1,0:T(4,128)S(1)}, s32[]{:T(128)}, f32[16,512,512]{2,1,0:T(8,128)}, f32[4,8192]{1,0:T(4,128)S(1)}, /*index=5*/s32[]{:T(128)}) %tuple.100), condition=%wide.region_7.9_spmd, body=%wide.region_4.0_spmd.sunk | while | flops 201359360 | bytes 17957020 | solution.py:68
  1091.2 199.8 %collective-permute-done.1 = f32[4,8192]{1,0:T(4,128)S(1)} collective-permute-done((f32[4,8192]{1,0:T(4,128)S(1)}, f32[4,8192]{1,0:T(4,128)S(1)}, u32[]{:S(2)}, u32[]{:S(2)}) %collective-permute-start.1) | collective-permute-done | bytes 131104 | tf_op jit(solution)/shard_map/while/body/eval_jaxpr/ppermute | solution.py:29
  1291.0 17.3 %conditional.5 = (f32[4,8192]{1,0:T(4,128)S(1)}) conditional(s32[]{:T(128)} %convert_element_type.56, f32[4,8192]{1,0:T(4,128)S(1)} %get-tuple-element.399, (f32[4,8192]{1,0:T(4,128)S(1)}, f32[16,512,512]{2,1,0:T(8,128)}, f32[4,8192]{1,0:T(4,128)S(1)}) %tuple.87), branch_computations={%region_5.6_spmd, %region_6.7_spmd} | conditional | flops 201359360 | bytes 17432584 | solution.py:65
  1291.0 17.2 %fusion.68 = f32[16,4,512]{2,1,0:T(4,128)S(1)} fusion(f32[4,16,512]{2,0,1:T(4,128)S(1)} %bitcast.166, f32[16,512,512]{2,1,0:T(8,128)} %get-tuple-element.235), kind=kOutput, calls=%fused_computation.99 | convolution fusion | flops 201326592 | bytes 17039360 | tf_op jit(solution)/shard_map/while/body/eval_jaxpr/cond/branch_1_fun/rab,trb->tra/dot_general | solution.py:36
  (258 shorter events, 469.0 us)
Async XLA Ops:
  102.2 9.3 collective-permute-start
  111.5 10.5 collective-permute-start
  122.0 10.6 collective-permute-start
  132.6 10.6 collective-permute-start
  143.2 10.6 collective-permute-start
  153.7 10.6 collective-permute-start
  164.3 10.6 collective-permute-start
  174.9 10.6 collective-permute-start
  185.5 10.6 collective-permute-start
  196.1 10.6 collective-permute-start
  206.7 10.6 collective-permute-start
  217.3 10.6 collective-permute-start
  227.9 9.4 collective-permute-start
  237.3 9.3 collective-permute-start
  246.6 9.3 collective-permute-start
  255.9 9.3 collective-permute-start
  293.0 395.3 %collective-permute-start = (f32[4,8192]{1,0:T(4,128)S(1)}, f32[4,8192]{1,0:T(4,128)S(1)}, u32[]{:S(2)}, u32[]{:S(2)}) collective-permute-start(f32[4,8192]{1,0:T(4,128)S(1)} %get-tuple-element.380), channel_id=1, source_target_pairs={{0,8},{8,16},{16,24},{24,32},{32,40},{40,48},{48,56},{56,64},{64,7... | collective-permute-start | bytes 393224 | tf_op jit(solution)/shard_map/while/body/eval_jaxpr/ppermute | solution.py:29
  844.2 21.0 %collective-permute-start.16 = (bf16[4,2,512]{2,0,1:T(4,128)(2,1)S(1)}, bf16[4,2,512]{2,0,1:T(4,128)(2,1)S(1)}, u32[]{:S(2)}, u32[]{:S(2)}) collective-permute-start(bf16[4,2,512]{2,0,1:T(4,128)(2,1)S(1)} %get-tuple-element.279), channel_id=1, source_target_pairs={{0,1},{1,2},{2,3},{3,4},{4,5},{5,6},{6,7},{7,0},{8,9},{9,10},{10,1... | collective-permute-start | bytes 24584 | tf_op jit(solution)/shard_map/ppermute | solution.py:17
  844.4 20.9 %collective-permute-start.17 = (bf16[4,2,512]{2,0,1:T(4,128)(2,1)S(1)}, bf16[4,2,512]{2,0,1:T(4,128)(2,1)S(1)}, u32[]{:S(2)}, u32[]{:S(2)}) collective-permute-start(bf16[4,2,512]{2,0,1:T(4,128)(2,1)S(1)} %get-tuple-element.280), channel_id=1, source_target_pairs={{1,0},{2,1},{3,2},{4,3},{5,4},{6,5},{7,6},{0,7},{9,8},{10,9},{11,1... | collective-permute-start | bytes 24584 | tf_op jit(solution)/shard_map/ppermute | solution.py:19
  1042.1 9.3 collective-permute-start.1
  1051.4 10.5 collective-permute-start.1
  1061.9 9.4 collective-permute-start.1
  1071.3 9.3 collective-permute-start.1
  1089.9 201.1 %collective-permute-start.1 = (f32[4,8192]{1,0:T(4,128)S(1)}, f32[4,8192]{1,0:T(4,128)S(1)}, u32[]{:S(2)}, u32[]{:S(2)}) collective-permute-start(f32[4,8192]{1,0:T(4,128)S(1)} %get-tuple-element.399), channel_id=1, source_target_pairs={{0,8},{8,16},{16,24},{24,32},{32,40},{40,48},{48,56},{56,64},{64,7... | collective-permute-start | bytes 393224 | tf_op jit(solution)/shard_map/while/body/eval_jaxpr/ppermute | solution.py:29
  (57 other events, 1023.9 us)
where the time goes:
time: 1320 us; the launch traced here: 1310 us
  waiting for transfers between devices  989 us (75%)
  matrix products  198 us (15%)
  starting transfers between devices  110 us (8%)
    ppermute x62, waiting for transfers between devices, shifted(): lax.ppermute(value, axis, [(source, source + steps) for source in range(f...  983 us
    dot_general x8, matrix products, fine_step(): jnp.einsum('rjab,trjb->tra', operator, picked, preferred_element_type=jnp...  112 us
    dot_general x5, matrix products, coarse_apply(): jnp.einsum('rab,trb->tra', matrix, stacked, precision=lax.Precision.HIGHEST)  86.1 us
    ppermute x62, starting transfers between devices, shifted(): lax.ppermute(value, axis, [(source, source + steps) for source in range(f...  79.4 us
    ppermute x8, starting transfers between devices, padded_2(): lax.ppermute(head, axis, [((i + 1) % count, i) for i in range(count)])  27.3 us
  transfers between devices with their start and end apart: 78, of which 69 were waited for; matrix products, arithmetic and copies ran while one was open for 1% of the time, Pallas kernels for 0%

commit v1 on v0

v1 whole, which is shorter than its diff:
```python
import functools

import jax
import jax.numpy as jnp
from jax import lax
from jax.experimental import pallas as pl
from jax.experimental.pallas import tpu as pltpu
from jax.sharding import PartitionSpec as P

MESH = pl.DeviceIdType.MESH
F32 = jnp.float32
BF16 = jnp.bfloat16

TRACERS = 4
BLK = 512
SLICES = 32
STEPS = 8
ROWS = 4
PAIR = 2
PIECE = PAIR * BLK
LANES = 128
LINES = PIECE // LANES
LEVELS = 4
CHUNK = 8


def slab_x(s, k):
    odd = lax.rem(s, 2)
    return 3 * odd + (1 - 2 * odd) * k


def dot(a, b):
    return jnp.dot(a, b, preferred_element_type=F32)


def halves(x):
    high = x.astype(BF16)
    return high, (x - high.astype(F32)).astype(BF16)


def kernel(
    initial_ref, sources_ref, operator_ref, cols_ref, coarse_ref, out_ref,
    coarse_vm, op_vm, opt_vm, high_vm, low_vm, init_vm, send_vm, recv_vm, osend_vm, orecv_vm,
    src_vm, v_vm, back_vm, end_vm, w_vm, halo_vm,
    load_sem, a2a_sem, hand_sem, send_sem, recv_sem,
):
    tm = lax.axis_index("tm")
    s = lax.axis_index("space")
    tracer = tm // 8
    x = lax.rem(tm // 2, 4)
    core = lax.rem(tm, 2)
    slab = slab_x(s, x)
    q = 2 * slab + core

    loads = [
        pltpu.make_async_copy(coarse_ref.at[pl.ds(ROWS * slab + PAIR * core, PAIR)], coarse_vm, load_sem.at[0]),
        pltpu.make_async_copy(
            initial_ref.at[:, pl.ds(pl.multiple_of(q * PIECE, PIECE), PIECE)], init_vm, load_sem.at[1]
        ),
        pltpu.make_async_copy(operator_ref.at[pl.ds(ROWS * slab, ROWS)], op_vm, load_sem.at[2]),
    ]
    for load in loads:
        load.start()

    barrier = pltpu.get_barrier_semaphore()

    def greet(j, carry):
        pl.semaphore_signal(barrier, inc=1, device_id=(lax.rem(tm + j, 32), s), device_id_type=MESH)
        return carry

    lax.fori_loop(1, 32, greet, 0)
    place = 4 * s + slab
    beside = []
    for step in (-1, 1):
        other = lax.rem(place + step + 32, 32)
        other_s = other // 4
        other_x = slab_x(other_s, lax.rem(other, 4))
        beside.append(((tracer * 4 + other_x) * 2 + 1, other_s))

    @pl.when(core == 1)
    def _():
        for other in beside:
            pl.semaphore_signal(barrier, inc=1, device_id=other, device_id_type=MESH)

    for piece in range(8):
        for line in range(LINES):
            at = piece * PIECE + line * LANES
            send_vm[4 * piece : 4 * piece + 4, line, :] = sources_ref[0, :, at : at + LANES]

    pl.semaphore_wait(barrier, 31 + 2 * core)

    def scatter(j, carry):
        to = lax.rem(tm + j, 32)
        to_q = 2 * slab_x(s, lax.rem(to // 2, 4)) + lax.rem(to, 2)
        pltpu.make_async_remote_copy(
            send_vm.at[to_q * 4 + to // 8], recv_vm.at[tm], a2a_sem.at[0], a2a_sem.at[1],
            device_id=(to, s), device_id_type=MESH,
        ).start()
        return carry

    lax.fori_loop(1, 32, scatter, 0)
    recv_vm[tm] = send_vm[q * 4 + tracer]

    loads[0].wait()
    for b in range(PAIR):
        high, low = halves(coarse_vm[b].T)
        high_vm[0, b] = high
        low_vm[0, b] = low

    def square(i, carry):
        level, b = i // PAIR, lax.rem(i, PAIR)
        high, low = high_vm[level, b], low_vm[level, b]
        high, low = halves(dot(high, high) + dot(high, low) + dot(low, high))
        high_vm[level + 1, b] = high
        low_vm[level + 1, b] = low
        return carry

    lax.fori_loop(0, PAIR * (LEVELS - 1), square, 0)

    loads[2].wait()

    def offset_of(i, j):
        row = ROWS * slab + i
        return lax.rem(cols_ref[row, j] - (16 * s + row) + 256, 128)

    def turn(i, carry):
        offsets = [offset_of(i, j) for j in range(4)]
        for slot in range(4):
            j = 0
            for other in range(1, 4):
                off = offsets[other]
                hit = off == (0, 127, 1)[slot] if slot < 3 else jnp.logical_or(off == 2, off == 126)
                j = jnp.where(hit, other, j)
            opt_vm[i, slot] = op_vm[i, j].T
        return carry

    lax.fori_loop(0, ROWS, turn, 0)

    def ahead(i):
        found = [(offset_of(i, j) == 2).astype(jnp.int32) for j in range(4)]
        return (found[0] + found[1] + found[2] + found[3]) > 0

    def all_pieces():
        return pltpu.make_async_remote_copy(
            send_vm.at[pl.ds(0, 31)], recv_vm.at[pl.ds(0, 31)], a2a_sem.at[0], a2a_sem.at[1],
            device_id=(tm, s), device_id_type=MESH,
        )

    loads[1].wait()
    all_pieces().wait_recv()
    all_pieces().wait_send()

    def coarse(level, value, b):
        rows = value.shape[0]
        high, low = value.astype(BF16).astype(F32), value
        both = jnp.concatenate([high, low - high], axis=0).astype(BF16)
        got = dot(both, high_vm[level, b]) + dot(both, low_vm[level, b])
        return got[:rows] + got[rows:]

    def scan(values, finish):
        for level in range(LEVELS - 1):
            by = 1 << level
            moved = [coarse(level, value, b) for b, value in enumerate(values)]
            values = [
                value + jnp.concatenate([jnp.zeros((by, BLK), F32), move[: SLICES - by]], axis=0)
                for value, move in zip(values, moved)
            ]
        last = [value[:CHUNK] for value in values]
        finish(0, last)
        for chunk in range(1, SLICES // CHUNK):
            last = [
                value[CHUNK * chunk : CHUNK * (chunk + 1)] + coarse(LEVELS - 1, before, b)
                for b, (value, before) in enumerate(zip(values, last))
            ]
            finish(chunk, last)

    first_row = lax.broadcasted_iota(jnp.int32, (SLICES, BLK), 0) == 0
    forced = []
    for b in range(PAIR):
        source = jnp.concatenate([recv_vm[:, 4 * b + line, :] for line in range(4)], axis=1)
        src_vm[PAIR * core + b] = source * (1.0 / STEPS)
        start = init_vm[pl.ds(tracer, 1), BLK * b : BLK * (b + 1)]
        forced.append(coarse(0, source + jnp.where(first_row, start, 0.0), b))

    def keep_end(chunk, last):
        for b in range(PAIR):
            end_vm[b, CHUNK * chunk : CHUNK * (chunk + 1)] = last[b]

    scan(forced, keep_end)
    for b in range(PAIR):
        start = init_vm[pl.ds(tracer, 1), BLK * b : BLK * (b + 1)]
        v_vm[PAIR * core + b] = jnp.concatenate([start, end_vm[b, : SLICES - 1]], axis=0)

    def hand(what, ref, to):
        return pltpu.make_async_remote_copy(
            ref.at[pl.ds(0, PAIR)], (v_vm, src_vm, back_vm)[what].at[pl.ds(0, PAIR)], hand_sem.at[what, 0], hand_sem.at[what, 1],
            device_id=(tm - core + to, s), device_id_type=MESH,
        )

    @pl.when(core == 0)
    def _():
        hand(0, v_vm, 1).start()
        hand(1, src_vm, 1).start()
        hand(0, v_vm, 1).wait_send()
        hand(1, src_vm, 1).wait_send()
        hand(2, v_vm, 1).wait_recv()

    @pl.when(core == 1)
    def _():
        hand(0, v_vm, 0).wait_recv()
        hand(1, src_vm, 0).wait_recv()

        def halo(parity, what):
            row = (0, 3, 1, 2)[what]
            return pltpu.make_async_remote_copy(
                w_vm.at[parity, row], halo_vm.at[parity, what], send_sem.at[parity, what],
                recv_sem.at[parity, what], device_id=beside[what % 2], device_id_type=MESH,
            )

        for row in (0, 3, 1, 2):
            w_vm[0, row] = v_vm[row].astype(BF16)
        for what in range(4):
            halo(0, what).start()
        signs = [ahead(i) for i in range(ROWS)]

        def fine(i, carry):
            now = lax.rem(i, 2)
            later = 1 - now
            w = [w_vm[now, row] for row in range(ROWS)]
            change = [
                dot(w[0], opt_vm[0, 0]) + dot(w[1], opt_vm[0, 2]),
                dot(w[0], opt_vm[1, 1]) + dot(w[1], opt_vm[1, 0]) + dot(w[2], opt_vm[1, 2]),
                dot(w[1], opt_vm[2, 1]) + dot(w[2], opt_vm[2, 0]) + dot(w[3], opt_vm[2, 2]),
                dot(w[2], opt_vm[3, 1]) + dot(w[3], opt_vm[3, 0]),
            ]

            @pl.when(i > 0)
            def _():
                for what in range(4):
                    halo(later, what).wait_send()

            halo(now, 1).wait_recv()
            left = halo_vm[now, 1]
            change[0] += dot(left, opt_vm[0, 1])
            halo(now, 0).wait_recv()
            right = halo_vm[now, 0]
            change[3] += dot(right, opt_vm[3, 2])
            halo(now, 3).wait_recv()
            change[0] += dot(jnp.where(signs[0], w[2], halo_vm[now, 3]), opt_vm[0, 3])
            halo(now, 2).wait_recv()
            change[3] += dot(jnp.where(signs[3], halo_vm[now, 2], w[1]), opt_vm[3, 3])
            for row in (0, 3):
                value = (v_vm[row] + change[row]) + src_vm[row]
                v_vm[row] = value
                w_vm[later, row] = value.astype(BF16)

            @pl.when(i < STEPS - 1)
            def _():
                halo(later, 0).start()
                halo(later, 1).start()

            change[1] += dot(jnp.where(signs[1], w[3], left), opt_vm[1, 3])
            change[2] += dot(jnp.where(signs[2], right, w[0]), opt_vm[2, 3])
            for row in (1, 2):
                value = (v_vm[row] + change[row]) + src_vm[row]
                v_vm[row] = value
                w_vm[later, row] = value.astype(BF16)

            @pl.when(i < STEPS - 1)
            def _():
                halo(later, 2).start()
                halo(later, 3).start()

            return carry

        lax.fori_loop(0, STEPS, fine, 0)
        for what in range(4):
            halo((STEPS - 1) % 2, what).wait_send()
        hand(2, v_vm, 0).start()
        hand(2, v_vm, 0).wait_send()

    def send_out(chunk, last):
        for b in range(PAIR):
            ends = end_vm[b, CHUNK * chunk : CHUNK * (chunk + 1)] + last[b]
            for line in range(4):
                osend_vm[CHUNK * chunk : CHUNK * (chunk + 1), 4 * b + line, :] = ends[:, LANES * line : LANES * (line + 1)]

        def one(j, carry):
            to = CHUNK * chunk + j

            @pl.when(to != tm)
            def _():
                pltpu.make_async_remote_copy(
                    osend_vm.at[to], orecv_vm.at[q * 4 + tracer], a2a_sem.at[2], a2a_sem.at[3],
                    device_id=(to, s), device_id_type=MESH,
                ).start()

            return carry

        lax.fori_loop(0, CHUNK, one, 0)

    scan([jnp.where(core == 0, back_vm[b], v_vm[PAIR + b]) - end_vm[b] for b in range(PAIR)], send_out)
    orecv_vm[q * 4 + tracer] = osend_vm[tm]
    back = pltpu.make_async_remote_copy(
        osend_vm.at[pl.ds(0, 31)], orecv_vm.at[pl.ds(0, 31)], a2a_sem.at[2], a2a_sem.at[3],
        device_id=(tm, s), device_id_type=MESH,
    )
    back.wait_recv()
    for piece in range(8):
        for line in range(LINES):
            at = piece * PIECE + line * LANES
            out_ref[0, :, at : at + LANES] = orecv_vm[4 * piece : 4 * piece + 4, line, :]
    back.wait_send()


def local(initial, sources, operator, col_blocks, coarse_inv):
    cells = initial.shape[1]
    return pl.pallas_call(
        kernel,
        out_shape=jax.ShapeDtypeStruct((1, TRACERS, cells), F32),
        in_specs=[
            pl.BlockSpec(memory_space=pl.ANY),
            pl.BlockSpec(memory_space=pltpu.VMEM),
            pl.BlockSpec(memory_space=pl.ANY),
            pl.BlockSpec(memory_space=pltpu.SMEM),
            pl.BlockSpec(memory_space=pl.ANY),
        ],
        out_specs=pl.BlockSpec(memory_space=pltpu.VMEM),
        scratch_shapes=[
            pltpu.VMEM((PAIR, BLK, BLK), F32),
            pltpu.VMEM((ROWS, 4, BLK, BLK), BF16),
            pltpu.VMEM((ROWS, 4, BLK, BLK), BF16),
            pltpu.VMEM((LEVELS, PAIR, BLK, BLK), BF16),
            pltpu.VMEM((LEVELS, PAIR, BLK, BLK), BF16),
            pltpu.VMEM((TRACERS, PIECE), F32),
            pltpu.VMEM((SLICES, LINES, LANES), F32),
            pltpu.VMEM((SLICES, LINES, LANES), F32),
            pltpu.VMEM((SLICES, LINES, LANES), F32),
            pltpu.VMEM((SLICES, LINES, LANES), F32),
            pltpu.VMEM((ROWS, SLICES, BLK), F32),
            pltpu.VMEM((ROWS, SLICES, BLK), F32),
            pltpu.VMEM((PAIR, SLICES, BLK), F32),
            pltpu.VMEM((PAIR, SLICES, BLK), F32),
            pltpu.VMEM((2, ROWS, SLICES, BLK), BF16),
            pltpu.VMEM((2, ROWS, SLICES, BLK), BF16),
            pltpu.SemaphoreType.DMA((3,)),
            pltpu.SemaphoreType.DMA((4,)),
            pltpu.SemaphoreType.DMA((3, 2)),
            pltpu.SemaphoreType.DMA((2, 4)),
            pltpu.SemaphoreType.DMA((2, 4)),
        ],
        compiler_params=pltpu.CompilerParams(
            collective_id=0, has_side_effects=True, vmem_limit_bytes=50 << 20
        ),
        name="parareal",
    )(initial, sources, operator, col_blocks, coarse_inv)


def solution(mesh):
    placed = (
        P(None, "space"),
        P("tm", None, "space"),
        P("space", None, None, None),
        P("space", None),
        P("space", None, None),
    )
    return jax.shard_map(
        local, mesh=mesh, in_specs=placed, out_specs=P("tm", None, "space"), check_vma=False
    )
```

time: 1320 us -> 66.1 us (0.05)
  the two profiles are of different devices: /device:TPU:231 before, /device:TPU:1 now
where the time goes in v1:
time: 66.1 us; the launch traced here: 65.1 us
  Pallas kernels  61.9 us (94%)
  local copies, waits for them, and re-layouts  3.22 us (5%)
    pallas_call x1, Pallas kernels, local(): pl.pallas_call(kernel, out_shape=jax.ShapeDtypeStruct((1, TRACERS, cells)...  61.9 us
    unnamed x6, local copies, waits for them, and re-layouts  3.22 us

profile of v1, /device:TPU:1, one launch (start us, length us, event | category | flops | bytes accessed | tf_op | source)
XLA Modules:
  0.0 65.1 jit_solution(14255473451838601407)
XLA Ops:
  0.0 0.8 %copy.6.cols_ref = s32[16,4]{1,0:T(8,128)S(1)} copy(s32[16,4]{0,1:T(4,128)} %param.8) | data formatting | bytes 512 | tf_op args[3]
  0.8 0.0 copy-start
  0.8 0.9 %copy-done = f32[4,8192]{1,0:T(4,128)S(1)} copy-done((f32[4,8192]{1,0:T(4,128)S(1)}, f32[4,8192]{1,0:T(4,128)}, u32[]{:S(2)}) %copy-start) | copy-done | bytes 131096
  1.7 0.0 copy-start.1
  1.7 0.9 %copy-done.1 = f32[1,4,8192]{2,1,0:T(4,128)S(1)} copy-done((f32[1,4,8192]{2,1,0:T(4,128)S(1)}, f32[1,4,8192]{2,1,0:T(4,128)}, u32[]{:S(2)}) %copy-start.1) | copy-done | bytes 131096
  2.6 61.9 %parareal.1 = f32[1,4,8192]{2,1,0:T(4,128)S(1)} custom-call(f32[4,8192]{1,0:T(4,128)S(1)} %copy-done, f32[1,4,8192]{2,1,0:T(4,128)S(1)} %copy-done.1, bf16[16,4,512,512]{3,2,1,0:T(8,128)(2,1)} %operator_ref.1, s32[16,4]{1,0:T(8,128)S(1)} %copy.6.cols_ref, f32[16,512,512]{2,1,0:T(8,128)} %coarse_ref.1), custom_call_target="tpu_custom_call" | custom-call | tf_op jit(solution)/shard_map/parareal/pallas_call | solution.py:318
  64.5 0.7 %copy.8 = f32[1,4,8192]{2,1,0:T(4,128)} copy(f32[1,4,8192]{2,1,0:T(4,128)S(1)} %parareal.1) | data formatting | bytes 262144
Async XLA Ops:
  0.8 0.9 %copy-start = (f32[4,8192]{1,0:T(4,128)S(1)}, f32[4,8192]{1,0:T(4,128)}, u32[]{:S(2)}) copy-start(f32[4,8192]{1,0:T(4,128)} %initial_ref.1) | copy-start | bytes 393220
  1.7 0.9 %copy-start.1 = (f32[1,4,8192]{2,1,0:T(4,128)S(1)}, f32[1,4,8192]{2,1,0:T(4,128)}, u32[]{:S(2)}) copy-start(f32[1,4,8192]{2,1,0:T(4,128)} %sources_ref.1) | copy-start | bytes 393220

commit v2 on v1

v2 whole, which is shorter than its diff:
```python
import jax
import jax.numpy as jnp
from jax import lax
from jax.experimental import pallas as pl
from jax.experimental.pallas import tpu as pltpu
from jax.sharding import PartitionSpec as P

MESH = pl.DeviceIdType.MESH
F32 = jnp.float32
BF16 = jnp.bfloat16

TRACERS = 4
BLK = 512
SLICES = 32
STEPS = 8
ROWS = 4
PAIR = 2
PIECE = PAIR * BLK
LANES = 128
LINES = PIECE // LANES
LEVELS = 4
CHUNK = 8
PART = 16
PARTS = SLICES // PART


def slab_x(s, k):
    odd = lax.rem(s, 2)
    return 3 * odd + (1 - 2 * odd) * k


def dot(a, b):
    return jnp.dot(a, b, preferred_element_type=F32)


def halves(x):
    high = x.astype(BF16)
    return high, (x - high.astype(F32)).astype(BF16)


def kernel(
    initial_ref, sources_ref, operator_ref, cols_ref, coarse_ref, out_ref,
    source_vm, cols_sm, coarse_vm, op_vm, opt_vm, high_vm, low_vm, init_vm, send_vm, recv_vm, osend_vm, orecv_vm,
    src_vm, v_vm, back_vm, end_vm, w_vm, halo_vm,
    load_sem, a2a_sem, hand_sem, send_sem, recv_sem,
):
    tm = lax.axis_index("tm")
    s = lax.axis_index("space")
    tracer = tm // 8
    inner = lax.rem(tm, 8)
    x = inner // 2
    core = lax.rem(tm, 2)
    slab = slab_x(s, x)
    q = 2 * slab + core

    barrier = pltpu.get_barrier_semaphore()

    def others(do):
        for away in (2, 1, 3, 0):
            base = 8 * lax.rem(tracer + away, 4)

            def one(j, carry):
                do(base + lax.rem(inner + j, 8))
                return carry

            lax.fori_loop(1 if away == 0 else 0, 8, one, 0)

    def greet(to):
        pl.semaphore_signal(barrier, inc=1, device_id=to, device_id_type=MESH)

    place = 4 * s + slab
    beside = []
    for step in (-1, 1):
        other = lax.rem(place + step + 32, 32)
        other_s = other // 4
        other_x = slab_x(other_s, lax.rem(other, 4))
        beside.append(((tracer * 4 + other_x) * 2 + 1, other_s))

    greet(beside[0])

    @pl.when(core == 1)
    def _():
        greet(beside[1])
        greet((beside[1][0] - 1, beside[1][1]))

    others(lambda to: greet((to, s)))

    load_sources = pltpu.make_async_copy(sources_ref.at[0], source_vm, load_sem.at[0])
    load_coarse = pltpu.make_async_copy(
        coarse_ref.at[pl.ds(ROWS * slab + PAIR * core, PAIR)], coarse_vm, load_sem.at[1]
    )
    load_initial = pltpu.make_async_copy(
        initial_ref.at[:, pl.ds(pl.multiple_of(q * PIECE, PIECE), PIECE)], init_vm, load_sem.at[2]
    )
    load_cols = pltpu.make_async_copy(cols_ref, cols_sm, load_sem.at[3])
    load_operator = pltpu.make_async_copy(operator_ref.at[pl.ds(ROWS * slab, ROWS)], op_vm, load_sem.at[4])
    for load in (load_sources, load_coarse, load_initial, load_cols, load_operator):
        load.start()

    load_sources.wait()
    for piece in range(8):
        for line in range(LINES):
            at = piece * PIECE + line * LANES
            send_vm[4 * piece : 4 * piece + 4, line, :] = source_vm[:, at : at + LANES]
    recv_vm[tm] = send_vm[q * 4 + tracer]

    load_coarse.wait()
    for b in range(PAIR):
        high, low = halves(coarse_vm[b].T)
        high_vm[0, b] = high
        low_vm[0, b] = low

    def square(i):
        level, b = i // PAIR, lax.rem(i, PAIR)
        high, low = high_vm[level, b], low_vm[level, b]
        high, low = halves(dot(high, high) + dot(high, low) + dot(low, high))
        high_vm[level + 1, b] = high
        low_vm[level + 1, b] = low

    pl.semaphore_wait(barrier, 32 + 2 * core)

    def scatter(to):
        to_q = 2 * slab_x(s, lax.rem(to // 2, 4)) + lax.rem(to, 2)
        pltpu.make_async_remote_copy(
            send_vm.at[to_q * 4 + to // 8], recv_vm.at[tm], a2a_sem.at[0], a2a_sem.at[1],
            device_id=(to, s), device_id_type=MESH,
        ).start()

    others(scatter)

    load_cols.wait()
    load_operator.wait()

    def offset_of(i, j):
        row = ROWS * slab + i
        return lax.rem(cols_sm[j, row] - (16 * s + row) + 256, 128)

    def turn(i):
        offsets = [offset_of(i, j) for j in range(4)]
        for slot in range(4):
            j = 0
            for other in range(1, 4):
                off = offsets[other]
                hit = off == (0, 127, 1)[slot] if slot < 3 else jnp.logical_or(off == 2, off == 126)
                j = jnp.where(hit, other, j)
            opt_vm[i, slot] = op_vm[i, j].T

    def late(i, carry):
        square(i)
        turn(i)
        return carry

    lax.fori_loop(0, ROWS, late, 0)

    def ahead(i):
        found = [(offset_of(i, j) == 2).astype(jnp.int32) for j in range(4)]
        return (found[0] + found[1] + found[2] + found[3]) > 0

    def all_pieces():
        return pltpu.make_async_remote_copy(
            send_vm.at[pl.ds(0, 31)], recv_vm.at[pl.ds(0, 31)], a2a_sem.at[0], a2a_sem.at[1],
            device_id=(tm, s), device_id_type=MESH,
        )

    load_initial.wait()
    all_pieces().wait_recv()

    def coarse(level, value, b):
        rows = value.shape[0]
        high, low = value.astype(BF16).astype(F32), value
        both = jnp.concatenate([high, low - high], axis=0).astype(BF16)
        got = dot(both, high_vm[level, b]) + dot(both, low_vm[level, b])
        return got[:rows] + got[rows:]

    def scan(values, leap, finish):
        for level in range(LEVELS - 1):
            by = 1 << level
            moved = [coarse(level, value, b) for b, value in enumerate(values)]
            values = [
                value + jnp.concatenate([jnp.zeros((by, BLK), F32), move[: SLICES - by]], axis=0)
                for value, move in zip(values, moved)
            ]
        last = [value[:CHUNK] for value in values]
        finish(0, last)
        for chunk in range(1, SLICES // CHUNK):
            last = [
                value[CHUNK * chunk : CHUNK * (chunk + 1)] + leap(before, b)
                for b, (value, before) in enumerate(zip(values, last))
            ]
            finish(chunk, last)

    first_row = lax.broadcasted_iota(jnp.int32, (SLICES, BLK), 0) == 0
    forced = []
    for b in range(PAIR):
        source = jnp.concatenate([recv_vm[:, 4 * b + line, :] for line in range(4)], axis=1)
        src_vm[PAIR * core + b] = source * (1.0 / STEPS)
        start = init_vm[pl.ds(tracer, 1), BLK * b : BLK * (b + 1)]
        forced.append(coarse(0, source + jnp.where(first_row, start, 0.0), b))

    def keep_end(chunk, last):
        for b in range(PAIR):
            end_vm[b, CHUNK * chunk : CHUNK * (chunk + 1)] = last[b]

    def hand(what, ref, to):
        return pltpu.make_async_remote_copy(
            ref.at[pl.ds(0, PAIR)], (v_vm, src_vm, back_vm)[what].at[pl.ds(0, PAIR)], hand_sem.at[what, 0], hand_sem.at[what, 1],
            device_id=(tm - core + to, s), device_id_type=MESH,
        )

    def halo(parity, what, part):
        rows = pl.ds(PART * part, PART)
        return pltpu.make_async_remote_copy(
            w_vm.at[parity, (0, 3, 1, 2)[what], rows], halo_vm.at[parity, what, rows], send_sem.at[parity, what, part],
            recv_sem.at[parity, what, part], device_id=beside[what % 2], device_id_type=MESH,
        )

    @pl.when(core == 0)
    def _():
        hand(1, src_vm, 1).start()

    scan(forced, lambda before, b: coarse(2, coarse(2, before, b), b), keep_end)
    for b in range(PAIR):
        start = init_vm[pl.ds(tracer, 1), BLK * b : BLK * (b + 1)]
        start = jnp.concatenate([start, end_vm[b, : SLICES - 1]], axis=0)
        v_vm[PAIR * core + b] = start
        w_vm[0, PAIR * core + b] = start.astype(BF16)

    def last_powers():
        def one(b, carry):
            square(2 * PAIR + b)
            return carry

        lax.fori_loop(0, PAIR, one, 0)

    @pl.when(core == 0)
    def _():
        for part in range(PARTS):
            halo(0, 0, part).start()
            halo(0, 2, part).start()
        hand(0, v_vm, 1).start()
        last_powers()
        for part in range(PARTS):
            halo(0, 0, part).wait_send()
            halo(0, 2, part).wait_send()
        hand(0, v_vm, 1).wait_send()
        hand(1, src_vm, 1).wait_send()
        hand(2, v_vm, 1).wait_recv()

    @pl.when(core == 1)
    def _():
        for part in range(PARTS):
            halo(0, 1, part).start()
            halo(0, 3, part).start()
        last_powers()
        hand(0, v_vm, 0).wait_recv()
        for row in range(PAIR):
            w_vm[0, row] = v_vm[row].astype(BF16)
        hand(1, src_vm, 0).wait_recv()
        signs = [ahead(i) for i in range(ROWS)]

        def fine(i, carry):
            now = lax.rem(i, 2)
            later = 1 - now
            w = [w_vm[now, row] for row in range(ROWS)]
            inside = [
                dot(w[0], opt_vm[0, 0]) + dot(w[1], opt_vm[0, 2]),
                dot(w[0], opt_vm[1, 1]) + dot(w[1], opt_vm[1, 0]) + dot(w[2], opt_vm[1, 2]),
                dot(w[1], opt_vm[2, 1]) + dot(w[2], opt_vm[2, 0]) + dot(w[3], opt_vm[2, 2]),
                dot(w[2], opt_vm[3, 1]) + dot(w[3], opt_vm[3, 0]),
            ]

            @pl.when(i > 0)
            def _():
                for part in range(PARTS):
                    halo(later, 1, part).wait_send()
                    halo(later, 3, part).wait_send()

            @pl.when(i > 1)
            def _():
                for part in range(PARTS):
                    halo(later, 0, part).wait_send()
                    halo(later, 2, part).wait_send()

            for part in range(PARTS):
                at = slice(PART * part, PART * (part + 1))
                change = [value[at] for value in inside]

                def update(row):
                    value = (v_vm[row, at] + change[row]) + src_vm[row, at]
                    v_vm[row, at] = value
                    w_vm[later, row, at] = value.astype(BF16)

                halo(now, 1, part).wait_recv()
                left = halo_vm[now, 1, at]
                change[0] += dot(left, opt_vm[0, 1])
                halo(now, 0, part).wait_recv()
                right = halo_vm[now, 0, at]
                change[3] += dot(right, opt_vm[3, 2])
                halo(now, 3, part).wait_recv()
                change[0] += dot(jnp.where(signs[0], w[2][at], halo_vm[now, 3, at]), opt_vm[0, 3])
                halo(now, 2, part).wait_recv()
                change[3] += dot(jnp.where(signs[3], halo_vm[now, 2, at], w[1][at]), opt_vm[3, 3])
                update(0)
                update(3)

                @pl.when(i < STEPS - 1)
                def _():
                    halo(later, 0, part).start()
                    halo(later, 1, part).start()

                change[1] += dot(jnp.where(signs[1], w[3][at], left), opt_vm[1, 3])
                change[2] += dot(jnp.where(signs[2], right, w[0][at]), opt_vm[2, 3])
                update(1)
                update(2)

                @pl.when(i < STEPS - 1)
                def _():
                    halo(later, 2, part).start()
                    halo(later, 3, part).start()

            return carry

        lax.fori_loop(0, STEPS, fine, 0)
        for part in range(PARTS):
            for what in range(4):
                halo((STEPS - 1) % 2, what, part).wait_send()
        hand(2, v_vm, 0).start()
        hand(2, v_vm, 0).wait_send()

    def send_out(chunk, last):
        for b in range(PAIR):
            ends = end_vm[b, CHUNK * chunk : CHUNK * (chunk + 1)] + last[b]
            for line in range(4):
                osend_vm[CHUNK * chunk : CHUNK * (chunk + 1), 4 * b + line, :] = ends[:, LANES * line : LANES * (line + 1)]

        def one(j, carry):
            to = CHUNK * chunk + lax.rem(inner + j, CHUNK)

            @pl.when(to != tm)
            def _():
                pltpu.make_async_remote_copy(
                    osend_vm.at[to], orecv_vm.at[q * 4 + tracer], a2a_sem.at[2], a2a_sem.at[3],
                    device_id=(to, s), device_id_type=MESH,
                ).start()

            return carry

        lax.fori_loop(0, CHUNK, one, 0)

    scan([jnp.where(core == 0, back_vm[b], v_vm[PAIR + b]) - end_vm[b] for b in range(PAIR)], lambda before, b: coarse(3, before, b), send_out)
    orecv_vm[q * 4 + tracer] = osend_vm[tm]
    back = pltpu.make_async_remote_copy(
        osend_vm.at[pl.ds(0, 31)], orecv_vm.at[pl.ds(0, 31)], a2a_sem.at[2], a2a_sem.at[3],
        device_id=(tm, s), device_id_type=MESH,
    )
    back.wait_recv()
    for piece in range(8):
        for line in range(LINES):
            at = piece * PIECE + line * LANES
            out_ref[0, :, at : at + LANES] = orecv_vm[4 * piece : 4 * piece + 4, line, :]
    back.wait_send()
    all_pieces().wait_send()


def local(initial, sources, operator, col_blocks, coarse_inv):
    cells = initial.shape[1]
    cols = col_blocks.T
    return pl.pallas_call(
        kernel,
        out_shape=pltpu.VMEM((1, TRACERS, cells), F32),
        in_specs=[
            pl.BlockSpec(memory_space=pltpu.HBM),
            pl.BlockSpec(memory_space=pltpu.HBM),
            pl.BlockSpec(memory_space=pltpu.HBM),
            pl.BlockSpec(memory_space=pltpu.HBM),
            pl.BlockSpec(memory_space=pltpu.HBM),
        ],
        out_specs=pl.BlockSpec(memory_space=pltpu.VMEM),
        scratch_shapes=[
            pltpu.VMEM((TRACERS, cells), F32),
            pltpu.SMEM(cols.shape, jnp.int32),
            pltpu.VMEM((PAIR, BLK, BLK), F32),
            pltpu.VMEM((ROWS, 4, BLK, BLK), BF16),
            pltpu.VMEM((ROWS, 4, BLK, BLK), BF16),
            pltpu.VMEM((LEVELS, PAIR, BLK, BLK), BF16),
            pltpu.VMEM((LEVELS, PAIR, BLK, BLK), BF16),
            pltpu.VMEM((TRACERS, PIECE), F32),
            pltpu.VMEM((SLICES, LINES, LANES), F32),
            pltpu.VMEM((SLICES, LINES, LANES), F32),
            pltpu.VMEM((SLICES, LINES, LANES), F32),
            pltpu.VMEM((SLICES, LINES, LANES), F32),
            pltpu.VMEM((ROWS, SLICES, BLK), F32),
            pltpu.VMEM((ROWS, SLICES, BLK), F32),
            pltpu.VMEM((PAIR, SLICES, BLK), F32),
            pltpu.VMEM((PAIR, SLICES, BLK), F32),
            pltpu.VMEM((2, ROWS, SLICES, BLK), BF16),
            pltpu.VMEM((2, ROWS, SLICES, BLK), BF16),
            pltpu.SemaphoreType.DMA((5,)),
            pltpu.SemaphoreType.DMA((4,)),
            pltpu.SemaphoreType.DMA((3, 2)),
            pltpu.SemaphoreType.DMA((2, 4, PARTS)),
            pltpu.SemaphoreType.DMA((2, 4, PARTS)),
        ],
        compiler_params=pltpu.CompilerParams(
            collective_id=0, has_side_effects=True, vmem_limit_bytes=63 << 20
        ),
        name="parareal",
    )(initial, sources, operator, cols, coarse_inv)


def solution(mesh):
    placed = (
        P(None, "space"),
        P("tm", None, "space"),
        P("space", None, None, None),
        P("space", None),
        P("space", None, None),
    )
    return jax.shard_map(
        local, mesh=mesh, in_specs=placed, out_specs=P("tm", None, "space"), check_vma=False
    )
```

time: 66.1 us -> 58.9 us (0.89); the launches traced: 65.1 us -> 58.8 us
  Pallas kernels: 61.9 us -> 58.2 us
  local copies, waits for them, and re-layouts: 3.22 us -> 0.66 us
    pallas_call x1, Pallas kernels: 61.9 us -> 58.2 us  [local(): pl.pallas_call(kernel, out_shape=pltpu.VMEM((1, TRACERS, cells), F32), in...]
    unnamed x6 -> x1, local copies, waits for them, and re-layouts: 3.22 us -> 0.66 us
where the time goes in v2:
time: 58.9 us; the launch traced here: 58.8 us
  Pallas kernels  58.2 us (99%)
  local copies, waits for them, and re-layouts  0.66 us (1%)
    pallas_call x1, Pallas kernels, local(): pl.pallas_call(kernel, out_shape=pltpu.VMEM((1, TRACERS, cells), F32), in...  58.2 us

profile of v2, /device:TPU:1, one launch (start us, length us, event | category | flops | bytes accessed | tf_op | source)
XLA Modules:
  0.0 58.8 jit_solution(13349096501161900996)
XLA Ops:
  0.0 58.2 %parareal.1 = f32[1,4,8192]{2,1,0:T(4,128)S(1)} custom-call(f32[4,8192]{1,0:T(4,128)} %initial_ref.1, f32[1,4,8192]{2,1,0:T(4,128)} %sources_ref.1, bf16[16,4,512,512]{3,2,1,0:T(8,128)(2,1)} %operator_ref.1, s32[4,16]{1,0:T(4,128)} %bitcast.1, f32[16,512,512]{2,1,0:T(8,128)} %coarse_ref.1), custom_call_target="tpu_custom_call" | custom-call | tf_op jit(solution)/shard_map/parareal/pallas_call | solution.py:368
  58.2 0.7 %copy.7 = f32[1,4,8192]{2,1,0:T(4,128)} copy(f32[1,4,8192]{2,1,0:T(4,128)S(1)} %parareal.1) | data formatting | bytes 262144

commit v3 on v2

--- a/solution.py
+++ b/solution.py
@@ -152,6 +152,12 @@
 
     lax.fori_loop(0, ROWS, late, 0)
 
+    def last(b, carry):
+        square(ROWS + b)
+        return carry
+
+    lax.fori_loop(0, PAIR, last, 0)
+
     def ahead(i):
         found = [(offset_of(i, j) == 2).astype(jnp.int32) for j in range(4)]
         return (found[0] + found[1] + found[2] + found[3]) > 0
@@ -172,7 +178,7 @@
         got = dot(both, high_vm[level, b]) + dot(both, low_vm[level, b])
         return got[:rows] + got[rows:]
 
-    def scan(values, leap, finish):
+    def scan(values, finish):
         for level in range(LEVELS - 1):
             by = 1 << level
             moved = [coarse(level, value, b) for b, value in enumerate(values)]
@@ -184,7 +190,7 @@
         finish(0, last)
         for chunk in range(1, SLICES // CHUNK):
             last = [
-                value[CHUNK * chunk : CHUNK * (chunk + 1)] + leap(before, b)
+                value[CHUNK * chunk : CHUNK * (chunk + 1)] + coarse(LEVELS - 1, before, b)
                 for b, (value, before) in enumerate(zip(values, last))
             ]
             finish(chunk, last)
@@ -218,19 +224,12 @@
     def _():
         hand(1, src_vm, 1).start()
 
-    scan(forced, lambda before, b: coarse(2, coarse(2, before, b), b), keep_end)
+    scan(forced, keep_end)
     for b in range(PAIR):
         start = init_vm[pl.ds(tracer, 1), BLK * b : BLK * (b + 1)]
         start = jnp.concatenate([start, end_vm[b, : SLICES - 1]], axis=0)
         v_vm[PAIR * core + b] = start
         w_vm[0, PAIR * core + b] = start.astype(BF16)
-
-    def last_powers():
-        def one(b, carry):
-            square(2 * PAIR + b)
-            return carry
-
-        lax.fori_loop(0, PAIR, one, 0)
 
     @pl.when(core == 0)
     def _():
@@ -238,7 +237,6 @@
             halo(0, 0, part).start()
             halo(0, 2, part).start()
         hand(0, v_vm, 1).start()
-        last_powers()
         for part in range(PARTS):
             halo(0, 0, part).wait_send()
             halo(0, 2, part).wait_send()
@@ -251,7 +249,6 @@
         for part in range(PARTS):
             halo(0, 1, part).start()
             halo(0, 3, part).start()
-        last_powers()
         hand(0, v_vm, 0).wait_recv()
         for row in range(PAIR):
             w_vm[0, row] = v_vm[row].astype(BF16)
@@ -281,42 +278,40 @@
                     halo(later, 0, part).wait_send()
                     halo(later, 2, part).wait_send()
 
-            for part in range(PARTS):
-                at = slice(PART * part, PART * (part + 1))
-                change = [value[at] for value in inside]
-
-                def update(row):
-                    value = (v_vm[row, at] + change[row]) + src_vm[row, at]
-                    v_vm[row, at] = value
-                    w_vm[later, row, at] = value.astype(BF16)
-
-                halo(now, 1, part).wait_recv()
-                left = halo_vm[now, 1, at]
-                change[0] += dot(left, opt_vm[0, 1])
-                halo(now, 0, part).wait_recv()
-                right = halo_vm[now, 0, at]
-                change[3] += dot(right, opt_vm[3, 2])
-                halo(now, 3, part).wait_recv()
-                change[0] += dot(jnp.where(signs[0], w[2][at], halo_vm[now, 3, at]), opt_vm[0, 3])
-                halo(now, 2, part).wait_recv()
-                change[3] += dot(jnp.where(signs[3], halo_vm[now, 2, at], w[1][at]), opt_vm[3, 3])
-                update(0)
-                update(3)
-
-                @pl.when(i < STEPS - 1)
-                def _():
-                    halo(later, 0, part).start()
-                    halo(later, 1, part).start()
-
-                change[1] += dot(jnp.where(signs[1], w[3][at], left), opt_vm[1, 3])
-                change[2] += dot(jnp.where(signs[2], right, w[0][at]), opt_vm[2, 3])
-                update(1)
-                update(2)
-
-                @pl.when(i < STEPS - 1)
-                def _():
-                    halo(later, 2, part).start()
-                    halo(later, 3, part).start()
+            for side in range(2):
+                edge, next_in = (0, 1) if side == 0 else (3, 2)
+                toward = 1 + side
+                for part in range(PARTS):
+                    at = slice(PART * part, PART * (part + 1))
+
+                    def update(row, change):
+                        value = (v_vm[row, at] + change) + src_vm[row, at]
+                        v_vm[row, at] = value
+                        w_vm[later, row, at] = value.astype(BF16)
+
+                    def send(what):
+                        @pl.when(i < STEPS - 1)
+                        def _():
+                            halo(later, what, part).start()
+
+                    halo(now, 1 - side, part).wait_recv()
+                    near = halo_vm[now, 1 - side, at]
+                    change = inside[edge][at] + dot(near, opt_vm[edge, toward])
+                    halo(now, 3 - side, part).wait_recv()
+                    far = halo_vm[now, 3 - side, at]
+                    out = signs[edge] if side == 1 else jnp.logical_not(signs[edge])
+                    update(edge, change + dot(jnp.where(out, far, w[3 - next_in][at]), opt_vm[edge, 3]))
+                    send(side)
+                    out = signs[next_in] if side == 1 else jnp.logical_not(signs[next_in])
+                    change = dot(jnp.where(out, near, w[3 - edge][at]), opt_vm[next_in, 3])
+                    update(next_in, inside[next_in][at] + change)
+                    send(2 + side)
+
+                if side == 0:
+
+                    @pl.when(i == STEPS - 1)
+                    def _():
+                        hand(2, v_vm, 0).start()
 
             return carry
 
@@ -324,7 +319,6 @@
         for part in range(PARTS):
             for what in range(4):
                 halo((STEPS - 1) % 2, what, part).wait_send()
-        hand(2, v_vm, 0).start()
         hand(2, v_vm, 0).wait_send()
 
     def send_out(chunk, last):
@@ -347,7 +341,7 @@
 
         lax.fori_loop(0, CHUNK, one, 0)
 
-    scan([jnp.where(core == 0, back_vm[b], v_vm[PAIR + b]) - end_vm[b] for b in range(PAIR)], lambda before, b: coarse(3, before, b), send_out)
+    scan([jnp.where(core == 0, back_vm[b], v_vm[PAIR + b]) - end_vm[b] for b in range(PAIR)], send_out)
     orecv_vm[q * 4 + tracer] = osend_vm[tm]
     back = pltpu.make_async_remote_copy(
         osend_vm.at[pl.ds(0, 31)], orecv_vm.at[pl.ds(0, 31)], a2a_sem.at[2], a2a_sem.at[3],

time: 58.9 us -> 57.3 us (0.973)
  Pallas kernels: 58.2 us -> 56.6 us
    pallas_call x1, Pallas kernels: 58.2 us -> 56.6 us  [local(): pl.pallas_call(kernel, out_shape=pltpu.VMEM((1, TRACERS, cells), F32), in...]
where the time goes in v3:
time: 57.3 us; the launch traced here: 57.2 us
  Pallas kernels  56.6 us (99%)
  local copies, waits for them, and re-layouts  0.66 us (1%)
    pallas_call x1, Pallas kernels, local(): pl.pallas_call(kernel, out_shape=pltpu.VMEM((1, TRACERS, cells), F32), in...  56.6 us

profile of v3, /device:TPU:1, one launch (start us, length us, event | category | flops | bytes accessed | tf_op | source)
XLA Modules:
  0.0 57.2 jit_solution(5741476351131008893)
XLA Ops:
  0.0 56.6 %parareal.1 = f32[1,4,8192]{2,1,0:T(4,128)S(1)} custom-call(f32[4,8192]{1,0:T(4,128)} %initial_ref.1, f32[1,4,8192]{2,1,0:T(4,128)} %sources_ref.1, bf16[16,4,512,512]{3,2,1,0:T(8,128)(2,1)} %operator_ref.1, s32[4,16]{1,0:T(4,128)} %bitcast.1, f32[16,512,512]{2,1,0:T(8,128)} %coarse_ref.1), custom_call_target="tpu_custom_call" | custom-call | tf_op jit(solution)/shard_map/parareal/pallas_call | solution.py:362
  56.6 0.7 %copy.7 = f32[1,4,8192]{2,1,0:T(4,128)} copy(f32[1,4,8192]{2,1,0:T(4,128)S(1)} %parareal.1) | data formatting | bytes 262144

commit v4 on v3

--- a/solution.py
+++ b/solution.py
@@ -53,6 +53,9 @@
     slab = slab_x(s, x)
     q = 2 * slab + core
 
+    load_sources = pltpu.make_async_copy(sources_ref.at[0], source_vm, load_sem.at[0])
+    load_sources.start()
+
     barrier = pltpu.get_barrier_semaphore()
 
     def others(do):
@@ -76,6 +79,7 @@
         other_x = slab_x(other_s, lax.rem(other, 4))
         beside.append(((tracer * 4 + other_x) * 2 + 1, other_s))
 
+    others(lambda to: greet((to, s)))
     greet(beside[0])
 
     @pl.when(core == 1)
@@ -83,9 +87,6 @@
         greet(beside[1])
         greet((beside[1][0] - 1, beside[1][1]))
 
-    others(lambda to: greet((to, s)))
-
-    load_sources = pltpu.make_async_copy(sources_ref.at[0], source_vm, load_sem.at[0])
     load_coarse = pltpu.make_async_copy(
         coarse_ref.at[pl.ds(ROWS * slab + PAIR * core, PAIR)], coarse_vm, load_sem.at[1]
     )
@@ -94,7 +95,7 @@
     )
     load_cols = pltpu.make_async_copy(cols_ref, cols_sm, load_sem.at[3])
     load_operator = pltpu.make_async_copy(operator_ref.at[pl.ds(ROWS * slab, ROWS)], op_vm, load_sem.at[4])
-    for load in (load_sources, load_coarse, load_initial, load_cols, load_operator):
+    for load in (load_coarse, load_initial, load_cols, load_operator):
         load.start()
 
     load_sources.wait()
@@ -126,7 +127,20 @@
             device_id=(to, s), device_id_type=MESH,
         ).start()
 
-    others(scatter)
+    for first, count in ((0, 2), (2, 6)):
+        for away in (2, 1, 3, 0):
+            base = 8 * lax.rem(tracer + away, 4) + first
+
+            def one(j, carry):
+                to = base + lax.rem(inner + j, count)
+
+                @pl.when(to != tm)
+                def _():
+                    scatter(to)
+
+                return carry
+
+            lax.fori_loop(0, count, one, 0)
 
     load_cols.wait()
     load_operator.wait()
@@ -203,10 +217,6 @@
         start = init_vm[pl.ds(tracer, 1), BLK * b : BLK * (b + 1)]
         forced.append(coarse(0, source + jnp.where(first_row, start, 0.0), b))
 
-    def keep_end(chunk, last):
-        for b in range(PAIR):
-            end_vm[b, CHUNK * chunk : CHUNK * (chunk + 1)] = last[b]
-
     def hand(what, ref, to):
         return pltpu.make_async_remote_copy(
             ref.at[pl.ds(0, PAIR)], (v_vm, src_vm, back_vm)[what].at[pl.ds(0, PAIR)], hand_sem.at[what, 0], hand_sem.at[what, 1],
@@ -224,18 +234,37 @@
     def _():
         hand(1, src_vm, 1).start()
 
+    def keep_end(chunk, last):
+        for b in range(PAIR):
+            end_vm[b, CHUNK * chunk : CHUNK * (chunk + 1)] = last[b]
+        done = CHUNK * (chunk + 1)
+        if done % PART:
+            return
+        part = done // PART - 1
+        for b in range(PAIR):
+            if part == 0:
+                start = init_vm[pl.ds(tracer, 1), BLK * b : BLK * (b + 1)]
+                start = jnp.concatenate([start, end_vm[b, : PART - 1]], axis=0)
+            else:
+                start = end_vm[b, PART * part - 1 : PART * (part + 1) - 1]
+            at = slice(PART * part, PART * (part + 1))
+            v_vm[PAIR * core + b, at] = start
+            w_vm[0, PAIR * core + b, at] = start.astype(BF16)
+
+        @pl.when(core == 0)
+        def _():
+            halo(0, 0, part).start()
+            halo(0, 2, part).start()
+
+        @pl.when(core == 1)
+        def _():
+            halo(0, 1, part).start()
+            halo(0, 3, part).start()
+
     scan(forced, keep_end)
-    for b in range(PAIR):
-        start = init_vm[pl.ds(tracer, 1), BLK * b : BLK * (b + 1)]
-        start = jnp.concatenate([start, end_vm[b, : SLICES - 1]], axis=0)
-        v_vm[PAIR * core + b] = start
-        w_vm[0, PAIR * core + b] = start.astype(BF16)
 
     @pl.when(core == 0)
     def _():
-        for part in range(PARTS):
-            halo(0, 0, part).start()
-            halo(0, 2, part).start()
         hand(0, v_vm, 1).start()
         for part in range(PARTS):
             halo(0, 0, part).wait_send()
@@ -246,9 +275,6 @@
 
     @pl.when(core == 1)
     def _():
-        for part in range(PARTS):
-            halo(0, 1, part).start()
-            halo(0, 3, part).start()
         hand(0, v_vm, 0).wait_recv()
         for row in range(PAIR):
             w_vm[0, row] = v_vm[row].astype(BF16)
@@ -278,11 +304,11 @@
                     halo(later, 0, part).wait_send()
                     halo(later, 2, part).wait_send()
 
-            for side in range(2):
-                edge, next_in = (0, 1) if side == 0 else (3, 2)
-                toward = 1 + side
-                for part in range(PARTS):
-                    at = slice(PART * part, PART * (part + 1))
+            for part in range(PARTS):
+                at = slice(PART * part, PART * (part + 1))
+                for side in range(2):
+                    edge, next_in = (0, 1) if side == 0 else (3, 2)
+                    toward = 1 + side
 
                     def update(row, change):
                         value = (v_vm[row, at] + change) + src_vm[row, at]
@@ -307,11 +333,11 @@
                     update(next_in, inside[next_in][at] + change)
                     send(2 + side)
 
-                if side == 0:
-
-                    @pl.when(i == STEPS - 1)
-                    def _():
-                        hand(2, v_vm, 0).start()
+                    if side == 0 and part == PARTS - 1:
+
+                        @pl.when(i == STEPS - 1)
+                        def _():
+                            hand(2, v_vm, 0).start()
 
             return carry
 

time: 57.3 us -> 55.7 us (0.972)
  Pallas kernels: 56.6 us -> 55 us
    pallas_call x1, Pallas kernels: 56.6 us -> 55 us  [local(): pl.pallas_call(kernel, out_shape=pltpu.VMEM((1, TRACERS, cells), F32), in...]
where the time goes in v4:
time: 55.7 us; the launch traced here: 55.6 us
  Pallas kernels  55 us (99%)
  local copies, waits for them, and re-layouts  0.66 us (1%)
    pallas_call x1, Pallas kernels, local(): pl.pallas_call(kernel, out_shape=pltpu.VMEM((1, TRACERS, cells), F32), in...  55 us

profile of v4, /device:TPU:1, one launch (start us, length us, event | category | flops | bytes accessed | tf_op | source)
XLA Modules:
  0.0 55.6 jit_solution(14987342594311260515)
XLA Ops:
  0.0 55.0 %parareal.1 = f32[1,4,8192]{2,1,0:T(4,128)S(1)} custom-call(f32[4,8192]{1,0:T(4,128)} %initial_ref.1, f32[1,4,8192]{2,1,0:T(4,128)} %sources_ref.1, bf16[16,4,512,512]{3,2,1,0:T(8,128)(2,1)} %operator_ref.1, s32[4,16]{1,0:T(4,128)} %bitcast.1, f32[16,512,512]{2,1,0:T(8,128)} %coarse_ref.1), custom_call_target="tpu_custom_call" | custom-call | tf_op jit(solution)/shard_map/parareal/pallas_call | solution.py:388
  55.0 0.7 %copy.7 = f32[1,4,8192]{2,1,0:T(4,128)} copy(f32[1,4,8192]{2,1,0:T(4,128)S(1)} %parareal.1) | data formatting | bytes 262144

commit v5 on v4

--- a/solution.py
+++ b/solution.py
@@ -29,6 +29,10 @@
     return 3 * odd + (1 - 2 * odd) * k
 
 
+def flipped(s):
+    return 1 - lax.rem(s, 4) // 2
+
+
 def dot(a, b):
     return jnp.dot(a, b, preferred_element_type=F32)
 
@@ -51,7 +55,13 @@
     x = inner // 2
     core = lax.rem(tm, 2)
     slab = slab_x(s, x)
-    q = 2 * slab + core
+    flip = flipped(s)
+    half = core + flip - 2 * core * flip
+    q = 2 * slab + half
+
+    def local_row(b):
+        return PAIR * core + b + flip * (1 - 2 * b)
+
 
     load_sources = pltpu.make_async_copy(sources_ref.at[0], source_vm, load_sem.at[0])
     load_sources.start()
@@ -72,12 +82,14 @@
         pl.semaphore_signal(barrier, inc=1, device_id=to, device_id_type=MESH)
 
     place = 4 * s + slab
-    beside = []
-    for step in (-1, 1):
-        other = lax.rem(place + step + 32, 32)
+    beside, their_side = [], []
+    for side in range(2):
+        other = lax.rem(place + (2 * side - 1) * (1 - 2 * flip) + 32, 32)
         other_s = other // 4
         other_x = slab_x(other_s, lax.rem(other, 4))
         beside.append(((tracer * 4 + other_x) * 2 + 1, other_s))
+        turned = flip + flipped(other_s) - 2 * flip * flipped(other_s)
+        their_side.append(1 - side + turned * (2 * side - 1))
 
     others(lambda to: greet((to, s)))
     greet(beside[0])
@@ -85,10 +97,14 @@
     @pl.when(core == 1)
     def _():
         greet(beside[1])
-        greet((beside[1][0] - 1, beside[1][1]))
+        for side in range(2):
+
+            @pl.when(their_side[side] == 0)
+            def _():
+                greet((beside[side][0] - 1, beside[side][1]))
 
     load_coarse = pltpu.make_async_copy(
-        coarse_ref.at[pl.ds(ROWS * slab + PAIR * core, PAIR)], coarse_vm, load_sem.at[1]
+        coarse_ref.at[pl.ds(ROWS * slab + PAIR * half, PAIR)], coarse_vm, load_sem.at[1]
     )
     load_initial = pltpu.make_async_copy(
         initial_ref.at[:, pl.ds(pl.multiple_of(q * PIECE, PIECE), PIECE)], init_vm, load_sem.at[2]
@@ -118,10 +134,11 @@
         high_vm[level + 1, b] = high
         low_vm[level + 1, b] = low
 
-    pl.semaphore_wait(barrier, 32 + 2 * core)
+    pl.semaphore_wait(barrier, 32 + core * (3 - their_side[0] - their_side[1]))
 
     def scatter(to):
-        to_q = 2 * slab_x(s, lax.rem(to // 2, 4)) + lax.rem(to, 2)
+        to_core = lax.rem(to, 2)
+        to_q = 2 * slab_x(s, lax.rem(to // 2, 4)) + to_core + flip - 2 * to_core * flip
         pltpu.make_async_remote_copy(
             send_vm.at[to_q * 4 + to // 8], recv_vm.at[tm], a2a_sem.at[0], a2a_sem.at[1],
             device_id=(to, s), device_id_type=MESH,
@@ -146,8 +163,8 @@
     load_operator.wait()
 
     def offset_of(i, j):
-        row = ROWS * slab + i
-        return lax.rem(cols_sm[j, row] - (16 * s + row) + 256, 128)
+        row = ROWS * slab + i + flip * (ROWS - 1 - 2 * i)
+        return lax.rem((cols_sm[j, row] - (16 * s + row)) * (1 - 2 * flip) + 256, 128)
 
     def turn(i):
         offsets = [offset_of(i, j) for j in range(4)]
@@ -157,7 +174,7 @@
                 off = offsets[other]
                 hit = off == (0, 127, 1)[slot] if slot < 3 else jnp.logical_or(off == 2, off == 126)
                 j = jnp.where(hit, other, j)
-            opt_vm[i, slot] = op_vm[i, j].T
+            opt_vm[i, slot] = op_vm[i + flip * (ROWS - 1 - 2 * i), j].T
 
     def late(i, carry):
         square(i)
@@ -213,7 +230,7 @@
     forced = []
     for b in range(PAIR):
         source = jnp.concatenate([recv_vm[:, 4 * b + line, :] for line in range(4)], axis=1)
-        src_vm[PAIR * core + b] = source * (1.0 / STEPS)
+        src_vm[local_row(b)] = source * (1.0 / STEPS)
         start = init_vm[pl.ds(tracer, 1), BLK * b : BLK * (b + 1)]
         forced.append(coarse(0, source + jnp.where(first_row, start, 0.0), b))
 
@@ -225,9 +242,17 @@
 
     def halo(parity, what, part):
         rows = pl.ds(PART * part, PART)
+        slot = what // 2 * 2 + their_side[what % 2]
         return pltpu.make_async_remote_copy(
-            w_vm.at[parity, (0, 3, 1, 2)[what], rows], halo_vm.at[parity, what, rows], send_sem.at[parity, what, part],
-            recv_sem.at[parity, what, part], device_id=beside[what % 2], device_id_type=MESH,
+            w_vm.at[parity, (0, 3, 1, 2)[what], rows], halo_vm.at[parity, slot, rows], send_sem.at[parity, what, part],
+            recv_sem.at[parity, slot, part], device_id=beside[what % 2], device_id_type=MESH,
+        )
+
+    def halo_in(parity, slot, part):
+        rows = pl.ds(PART * part, PART)
+        return pltpu.make_async_remote_copy(
+            w_vm.at[parity, slot, rows], halo_vm.at[parity, slot, rows], send_sem.at[parity, slot, part],
+            recv_sem.at[parity, slot, part], device_id=beside[slot % 2], device_id_type=MESH,
         )
 
     @pl.when(core == 0)
@@ -248,8 +273,8 @@
             else:
                 start = end_vm[b, PART * part - 1 : PART * (part + 1) - 1]
             at = slice(PART * part, PART * (part + 1))
-            v_vm[PAIR * core + b, at] = start
-            w_vm[0, PAIR * core + b, at] = start.astype(BF16)
+            v_vm[local_row(b), at] = start
+            w_vm[0, local_row(b), at] = start.astype(BF16)
 
         @pl.when(core == 0)
         def _():
@@ -320,11 +345,11 @@
                         def _():
                             halo(later, what, part).start()
 
-                    halo(now, 1 - side, part).wait_recv()
-                    near = halo_vm[now, 1 - side, at]
+                    halo_in(now, side, part).wait_recv()
+                    near = halo_vm[now, side, at]
                     change = inside[edge][at] + dot(near, opt_vm[edge, toward])
-                    halo(now, 3 - side, part).wait_recv()
-                    far = halo_vm[now, 3 - side, at]
+                    halo_in(now, 2 + side, part).wait_recv()
+                    far = halo_vm[now, 2 + side, at]
                     out = signs[edge] if side == 1 else jnp.logical_not(signs[edge])
                     update(edge, change + dot(jnp.where(out, far, w[3 - next_in][at]), opt_vm[edge, 3]))
                     send(side)
@@ -367,7 +392,11 @@
 
         lax.fori_loop(0, CHUNK, one, 0)
 
-    scan([jnp.where(core == 0, back_vm[b], v_vm[PAIR + b]) - end_vm[b] for b in range(PAIR)], send_out)
+    def result(b):
+        at = b + flip * (1 - 2 * b)
+        return jnp.where(core == 0, back_vm[at], v_vm[PAIR + at])
+
+    scan([result(b) - end_vm[b] for b in range(PAIR)], send_out)
     orecv_vm[q * 4 + tracer] = osend_vm[tm]
     back = pltpu.make_async_remote_copy(
         osend_vm.at[pl.ds(0, 31)], orecv_vm.at[pl.ds(0, 31)], a2a_sem.at[2], a2a_sem.at[3],

time: 55.7 us -> 54.8 us (0.984)
  Pallas kernels: 55 us -> 54 us
    pallas_call x1, Pallas kernels: 55 us -> 54 us  [local(): pl.pallas_call(kernel, out_shape=pltpu.VMEM((1, TRACERS, cells), F32), in...]
where the time goes in v5:
time: 54.8 us; the launch traced here: 54.7 us
  Pallas kernels  54 us (99%)
  local copies, waits for them, and re-layouts  0.66 us (1%)
    pallas_call x1, Pallas kernels, local(): pl.pallas_call(kernel, out_shape=pltpu.VMEM((1, TRACERS, cells), F32), in...  54 us

profile of v5, /device:TPU:1, one launch (start us, length us, event | category | flops | bytes accessed | tf_op | source)
XLA Modules:
  0.0 54.7 jit_solution(11124228986883179384)
XLA Ops:
  0.0 54.0 %parareal.1 = f32[1,4,8192]{2,1,0:T(4,128)S(1)} custom-call(f32[4,8192]{1,0:T(4,128)} %initial_ref.1, f32[1,4,8192]{2,1,0:T(4,128)} %sources_ref.1, bf16[16,4,512,512]{3,2,1,0:T(8,128)(2,1)} %operator_ref.1, s32[4,16]{1,0:T(4,128)} %bitcast.1, f32[16,512,512]{2,1,0:T(8,128)} %coarse_ref.1), custom_call_target="tpu_custom_call" | custom-call | tf_op jit(solution)/shard_map/parareal/pallas_call | solution.py:417
  54.0 0.7 %copy.7 = f32[1,4,8192]{2,1,0:T(4,128)} copy(f32[1,4,8192]{2,1,0:T(4,128)S(1)} %parareal.1) | data formatting | bytes 262144

commit v6 on v5

--- a/solution.py
+++ b/solution.py
@@ -22,6 +22,8 @@
 CHUNK = 8
 PART = 16
 PARTS = SLICES // PART
+SPAN = 256
+SPANS = BLK // SPAN
 
 
 def slab_x(s, k):
@@ -240,19 +242,19 @@
             device_id=(tm - core + to, s), device_id_type=MESH,
         )
 
-    def halo(parity, what, part):
-        rows = pl.ds(PART * part, PART)
+    def halo(parity, what, part, span):
+        rows, columns = pl.ds(PART * part, PART), pl.ds(SPAN * span, SPAN)
         slot = what // 2 * 2 + their_side[what % 2]
         return pltpu.make_async_remote_copy(
-            w_vm.at[parity, (0, 3, 1, 2)[what], rows], halo_vm.at[parity, slot, rows], send_sem.at[parity, what, part],
-            recv_sem.at[parity, slot, part], device_id=beside[what % 2], device_id_type=MESH,
+            w_vm.at[parity, (0, 3, 1, 2)[what], rows, columns], halo_vm.at[parity, slot, rows, columns], send_sem.at[parity, what, part, span],
+            recv_sem.at[parity, slot, part, span], device_id=beside[what % 2], device_id_type=MESH,
         )
 
-    def halo_in(parity, slot, part):
-        rows = pl.ds(PART * part, PART)
+    def halo_in(parity, slot, part, span):
+        rows, columns = pl.ds(PART * part, PART), pl.ds(SPAN * span, SPAN)
         return pltpu.make_async_remote_copy(
-            w_vm.at[parity, slot, rows], halo_vm.at[parity, slot, rows], send_sem.at[parity, slot, part],
-            recv_sem.at[parity, slot, part], device_id=beside[slot % 2], device_id_type=MESH,
+            w_vm.at[parity, slot, rows, columns], halo_vm.at[parity, slot, rows, columns], send_sem.at[parity, slot, part, span],
+            recv_sem.at[parity, slot, part, span], device_id=beside[slot % 2], device_id_type=MESH,
         )
 
     @pl.when(core == 0)
@@ -278,13 +280,17 @@
 
         @pl.when(core == 0)
         def _():
-            halo(0, 0, part).start()
-            halo(0, 2, part).start()
+            for span in range(SPANS):
+                halo(0, 0, part, span).start()
+            for span in range(SPANS):
+                halo(0, 2, part, span).start()
 
         @pl.when(core == 1)
         def _():
-            halo(0, 1, part).start()
-            halo(0, 3, part).start()
+            for span in range(SPANS):
+                halo(0, 1, part, span).start()
+            for span in range(SPANS):
+                halo(0, 3, part, span).start()
 
     scan(forced, keep_end)
 
@@ -292,8 +298,10 @@
     def _():
         hand(0, v_vm, 1).start()
         for part in range(PARTS):
-            halo(0, 0, part).wait_send()
-            halo(0, 2, part).wait_send()
+            for span in range(SPANS):
+                halo(0, 0, part, span).wait_send()
+            for span in range(SPANS):
+                halo(0, 2, part, span).wait_send()
         hand(0, v_vm, 1).wait_send()
         hand(1, src_vm, 1).wait_send()
         hand(2, v_vm, 1).wait_recv()
@@ -320,14 +328,18 @@
             @pl.when(i > 0)
             def _():
                 for part in range(PARTS):
-                    halo(later, 1, part).wait_send()
-                    halo(later, 3, part).wait_send()
+                    for span in range(SPANS):
+                        halo(later, 1, part, span).wait_send()
+                    for span in range(SPANS):
+                        halo(later, 3, part, span).wait_send()
 
             @pl.when(i > 1)
             def _():
                 for part in range(PARTS):
-                    halo(later, 0, part).wait_send()
-                    halo(later, 2, part).wait_send()
+                    for span in range(SPANS):
+                        halo(later, 0, part, span).wait_send()
+                    for span in range(SPANS):
+                        halo(later, 2, part, span).wait_send()
 
             for part in range(PARTS):
                 at = slice(PART * part, PART * (part + 1))
@@ -335,28 +347,29 @@
                     edge, next_in = (0, 1) if side == 0 else (3, 2)
                     toward = 1 + side
 
-                    def update(row, change):
-                        value = (v_vm[row, at] + change) + src_vm[row, at]
-                        v_vm[row, at] = value
-                        w_vm[later, row, at] = value.astype(BF16)
-
-                    def send(what):
-                        @pl.when(i < STEPS - 1)
-                        def _():
-                            halo(later, what, part).start()
-
-                    halo_in(now, side, part).wait_recv()
+                    def update(row, change, value, what):
+                        for span in range(SPANS):
+                            columns = slice(SPAN * span, SPAN * (span + 1))
+                            total = change[:, columns] + dot(value, opt_vm[row, 3, :, columns])
+                            total = (v_vm[row, at, columns] + total) + src_vm[row, at, columns]
+                            v_vm[row, at, columns] = total
+                            w_vm[later, row, at, columns] = total.astype(BF16)
+
+                            @pl.when(i < STEPS - 1)
+                            def _():
+                                halo(later, what, part, span).start()
+
+                    for span in range(SPANS):
+                        halo_in(now, side, part, span).wait_recv()
                     near = halo_vm[now, side, at]
                     change = inside[edge][at] + dot(near, opt_vm[edge, toward])
-                    halo_in(now, 2 + side, part).wait_recv()
+                    for span in range(SPANS):
+                        halo_in(now, 2 + side, part, span).wait_recv()
                     far = halo_vm[now, 2 + side, at]
                     out = signs[edge] if side == 1 else jnp.logical_not(signs[edge])
-                    update(edge, change + dot(jnp.where(out, far, w[3 - next_in][at]), opt_vm[edge, 3]))
-                    send(side)
+                    update(edge, change, jnp.where(out, far, w[3 - next_in][at]), side)
                     out = signs[next_in] if side == 1 else jnp.logical_not(signs[next_in])
-                    change = dot(jnp.where(out, near, w[3 - edge][at]), opt_vm[next_in, 3])
-                    update(next_in, inside[next_in][at] + change)
-                    send(2 + side)
+                    update(next_in, inside[next_in][at], jnp.where(out, near, w[3 - edge][at]), 2 + side)
 
                     if side == 0 and part == PARTS - 1:
 
@@ -369,7 +382,8 @@
         lax.fori_loop(0, STEPS, fine, 0)
         for part in range(PARTS):
             for what in range(4):
-                halo((STEPS - 1) % 2, what, part).wait_send()
+                for span in range(SPANS):
+                    halo((STEPS - 1) % 2, what, part, span).wait_send()
         hand(2, v_vm, 0).wait_send()
 
     def send_out(chunk, last):
@@ -447,8 +461,8 @@
             pltpu.SemaphoreType.DMA((5,)),
             pltpu.SemaphoreType.DMA((4,)),
             pltpu.SemaphoreType.DMA((3, 2)),
-            pltpu.SemaphoreType.DMA((2, 4, PARTS)),
-            pltpu.SemaphoreType.DMA((2, 4, PARTS)),
+            pltpu.SemaphoreType.DMA((2, 4, PARTS, SPANS)),
+            pltpu.SemaphoreType.DMA((2, 4, PARTS, SPANS)),
         ],
         compiler_params=pltpu.CompilerParams(
             collective_id=0, has_side_effects=True, vmem_limit_bytes=63 << 20

time: 54.8 us -> 64.1 us (1.17)
  Pallas kernels: 54 us -> 63.3 us
    pallas_call x1, Pallas kernels: 54 us -> 63.3 us  [local(): pl.pallas_call(kernel, out_shape=pltpu.VMEM((1, TRACERS, cells), F32), in...]
where the time goes in v6:
time: 64.1 us; the launch traced here: 64 us
  Pallas kernels  63.3 us (99%)
  local copies, waits for them, and re-layouts  0.66 us (1%)
    pallas_call x1, Pallas kernels, local(): pl.pallas_call(kernel, out_shape=pltpu.VMEM((1, TRACERS, cells), F32), in...  63.3 us

profile of v6, /device:TPU:1, one launch (start us, length us, event | category | flops | bytes accessed | tf_op | source)
XLA Modules:
  0.0 64.0 jit_solution(9952469924088591840)
XLA Ops:
  0.0 63.3 %parareal.1 = f32[1,4,8192]{2,1,0:T(4,128)S(1)} custom-call(f32[4,8192]{1,0:T(4,128)} %initial_ref.1, f32[1,4,8192]{2,1,0:T(4,128)} %sources_ref.1, bf16[16,4,512,512]{3,2,1,0:T(8,128)(2,1)} %operator_ref.1, s32[4,16]{1,0:T(4,128)} %bitcast.1, f32[16,512,512]{2,1,0:T(8,128)} %coarse_ref.1), custom_call_target="tpu_custom_call" | custom-call | tf_op jit(solution)/shard_map/parareal/pallas_call | solution.py:431
  63.3 0.7 %copy.7 = f32[1,4,8192]{2,1,0:T(4,128)} copy(f32[1,4,8192]{2,1,0:T(4,128)S(1)} %parareal.1) | data formatting | bytes 262144

commit v7 on v5

--- a/solution.py
+++ b/solution.py
@@ -240,19 +240,19 @@
             device_id=(tm - core + to, s), device_id_type=MESH,
         )
 
-    def halo(parity, what, part):
+    def halo(parity, side, part):
         rows = pl.ds(PART * part, PART)
-        slot = what // 2 * 2 + their_side[what % 2]
+        slot = their_side[side]
         return pltpu.make_async_remote_copy(
-            w_vm.at[parity, (0, 3, 1, 2)[what], rows], halo_vm.at[parity, slot, rows], send_sem.at[parity, what, part],
-            recv_sem.at[parity, slot, part], device_id=beside[what % 2], device_id_type=MESH,
+            w_vm.at[parity, pl.ds(PAIR * side, PAIR), rows], halo_vm.at[parity, slot, pl.ds(0, PAIR), rows],
+            send_sem.at[parity, side, part], recv_sem.at[parity, slot, part], device_id=beside[side], device_id_type=MESH,
         )
 
     def halo_in(parity, slot, part):
         rows = pl.ds(PART * part, PART)
         return pltpu.make_async_remote_copy(
-            w_vm.at[parity, slot, rows], halo_vm.at[parity, slot, rows], send_sem.at[parity, slot, part],
-            recv_sem.at[parity, slot, part], device_id=beside[slot % 2], device_id_type=MESH,
+            w_vm.at[parity, pl.ds(PAIR * slot, PAIR), rows], halo_vm.at[parity, slot, pl.ds(0, PAIR), rows],
+            send_sem.at[parity, slot, part], recv_sem.at[parity, slot, part], device_id=beside[slot], device_id_type=MESH,
         )
 
     @pl.when(core == 0)
@@ -279,12 +279,10 @@
         @pl.when(core == 0)
         def _():
             halo(0, 0, part).start()
-            halo(0, 2, part).start()
 
         @pl.when(core == 1)
         def _():
             halo(0, 1, part).start()
-            halo(0, 3, part).start()
 
     scan(forced, keep_end)
 
@@ -293,7 +291,6 @@
         hand(0, v_vm, 1).start()
         for part in range(PARTS):
             halo(0, 0, part).wait_send()
-            halo(0, 2, part).wait_send()
         hand(0, v_vm, 1).wait_send()
         hand(1, src_vm, 1).wait_send()
         hand(2, v_vm, 1).wait_recv()
@@ -321,13 +318,11 @@
             def _():
                 for part in range(PARTS):
                     halo(later, 1, part).wait_send()
-                    halo(later, 3, part).wait_send()
 
             @pl.when(i > 1)
             def _():
                 for part in range(PARTS):
                     halo(later, 0, part).wait_send()
-                    halo(later, 2, part).wait_send()
 
             for part in range(PARTS):
                 at = slice(PART * part, PART * (part + 1))
@@ -346,17 +341,15 @@
                             halo(later, what, part).start()
 
                     halo_in(now, side, part).wait_recv()
-                    near = halo_vm[now, side, at]
+                    near = halo_vm[now, side, their_side[side], at]
                     change = inside[edge][at] + dot(near, opt_vm[edge, toward])
-                    halo_in(now, 2 + side, part).wait_recv()
-                    far = halo_vm[now, 2 + side, at]
+                    far = halo_vm[now, side, 1 - their_side[side], at]
                     out = signs[edge] if side == 1 else jnp.logical_not(signs[edge])
                     update(edge, change + dot(jnp.where(out, far, w[3 - next_in][at]), opt_vm[edge, 3]))
-                    send(side)
                     out = signs[next_in] if side == 1 else jnp.logical_not(signs[next_in])
                     change = dot(jnp.where(out, near, w[3 - edge][at]), opt_vm[next_in, 3])
                     update(next_in, inside[next_in][at] + change)
-                    send(2 + side)
+                    send(side)
 
                     if side == 0 and part == PARTS - 1:
 
@@ -368,7 +361,7 @@
 
         lax.fori_loop(0, STEPS, fine, 0)
         for part in range(PARTS):
-            for what in range(4):
+            for what in range(2):
                 halo((STEPS - 1) % 2, what, part).wait_send()
         hand(2, v_vm, 0).wait_send()
 
@@ -443,12 +436,12 @@
             pltpu.VMEM((PAIR, SLICES, BLK), F32),
             pltpu.VMEM((PAIR, SLICES, BLK), F32),
             pltpu.VMEM((2, ROWS, SLICES, BLK), BF16),
-            pltpu.VMEM((2, ROWS, SLICES, BLK), BF16),
+            pltpu.VMEM((2, 2, PAIR, SLICES, BLK), BF16),
             pltpu.SemaphoreType.DMA((5,)),
             pltpu.SemaphoreType.DMA((4,)),
             pltpu.SemaphoreType.DMA((3, 2)),
-            pltpu.SemaphoreType.DMA((2, 4, PARTS)),
-            pltpu.SemaphoreType.DMA((2, 4, PARTS)),
+            pltpu.SemaphoreType.DMA((2, 2, PARTS)),
+            pltpu.SemaphoreType.DMA((2, 2, PARTS)),
         ],
         compiler_params=pltpu.CompilerParams(
             collective_id=0, has_side_effects=True, vmem_limit_bytes=63 << 20

time: 54.8 us -> 55.6 us (1.015)
  no operation moved by 1% of the time
where the time goes in v7:
time: 55.6 us; the launch traced here: 55 us
  Pallas kernels  54.4 us (98%)
  local copies, waits for them, and re-layouts  0.66 us (1%)
    pallas_call x1, Pallas kernels, local(): pl.pallas_call(kernel, out_shape=pltpu.VMEM((1, TRACERS, cells), F32), in...  54.4 us

profile of v7, /device:TPU:1, one launch (start us, length us, event | category | flops | bytes accessed | tf_op | source)
XLA Modules:
  0.0 55.0 jit_solution(2010848178261696111)
XLA Ops:
  0.0 54.4 %parareal.1 = f32[1,4,8192]{2,1,0:T(4,128)S(1)} custom-call(f32[4,8192]{1,0:T(4,128)} %initial_ref.1, f32[1,4,8192]{2,1,0:T(4,128)} %sources_ref.1, bf16[16,4,512,512]{3,2,1,0:T(8,128)(2,1)} %operator_ref.1, s32[4,16]{1,0:T(4,128)} %bitcast.1, f32[16,512,512]{2,1,0:T(8,128)} %coarse_ref.1), custom_call_target="tpu_custom_call" | custom-call | tf_op jit(solution)/shard_map/parareal/pallas_call | solution.py:410
  54.4 0.7 %copy.7 = f32[1,4,8192]{2,1,0:T(4,128)} copy(f32[1,4,8192]{2,1,0:T(4,128)S(1)} %parareal.1) | data formatting | bytes 262144
